TPU v7x, 256 devices: a whole 4x4x8 slice. The times are simulated.
256 devices in a mesh: dp: 16 (over z, core), tensor: 16 (over y, x).
Axes of the slice: x: 4, y: 4, z: 8, core: 2. Of those that a mesh axis runs over, the one named last changes fastest.
Arguments:
- activations: bfloat16 [36864, 8192], P('dp', 'tensor'), may hold values from -6 to 6
- out_grads: bfloat16 [36864, 28672], P('dp', 'tensor'), may hold values from -0.0546875 to 0.0546875
- basis: bfloat16 [8192, 256], P('tensor'), may hold values from -0.375 to 0.375
- first_moment: float32 [256, 28672], P('dp', 'tensor'), may hold values from -6 to 6
- second_moment: float32 [256, 28672], P('dp', 'tensor'), may hold values from 0.05 to 0.8
- reward_codes: int32 [36864], P('dp'), may hold values from 0 to 15
- token_ids: int32 [36864], P('dp'), may hold values from 0 to 128004, as said below
Outputs:
- new_first: float32 [256, 28672], P('dp', 'tensor')
- new_second: float32 [256, 28672], P('dp', 'tensor')
- weight_update: bfloat16 [8192, 28672], P('dp', 'tensor')
Inputs may be any that keep to these rules, and one draw needn't show every extreme that they name: `token_ids`: the id 128004 is the padding token; the first of each 2304 consecutive tokens is never padding.
All inputs are finite; a program needn't handle non-finite values.
Results may differ from a plain program's by a relative error of at most 0.019.
Values may be sent and summed in bfloat16 or wider, within the bound.
A program may use at most 64 MiB of HBM per device.

v0:
```python
import jax
import jax.numpy as jnp
from jax import lax
from jax.sharding import PartitionSpec as P

ADAM_STEP = 100
pad_token = 128004
reward_temp = 0.2
beta_one = 0.9
beta_two = 0.999
adam_eps = 1e-08


def filled_up(lines, size):
    spare = -len(lines) % size
    return jnp.pad(lines, [(0, spare)] + [(0, 0)] * (lines.ndim - 1))


def joined_along(parts, dim):
    parts = jnp.moveaxis(parts, 0, dim)
    lengths = parts.shape
    return parts.reshape(*lengths[:dim], lengths[dim] * lengths[dim + 1], *lengths[dim + 2 :])


def sent_to_all(shard, axis):
    size = lax.axis_size(axis)
    return lax.all_to_all(
        jnp.broadcast_to(shard[None], (size, *shard.shape)), axis, 0, 0, tiled=True
    )


def gather_directly(shard, axis, dim):
    return joined_along(sent_to_all(shard, axis), dim)


def split_up(shard, dim, size):
    before, after = (shard.shape[:dim], shard.shape[dim + 1 :])
    return jnp.moveaxis(shard.reshape(*before, size, -1, *after), dim, 0)


def sum_at_owner(shard, axis, dim):
    parts = split_up(shard, dim, lax.axis_size(axis))
    arrived = lax.all_to_all(parts, axis, split_axis=0, concat_axis=0, tiled=True)
    return arrived.astype(jnp.float32).sum(axis=0)


def total_of(shard, axes):
    lines = shard.reshape(-1, shard.shape[-1])
    padded = filled_up(lines, lax.axis_size(axes))
    whole = gather_directly(sum_at_owner(padded, axes, 0).astype(jnp.bfloat16), axes, 0)
    return lax.slice_in_dim(whole, 0, len(lines)).reshape(shard.shape).astype(jnp.float32)


def of_everyone(shard, axis):
    return sent_to_all(shard, axis).sum(axis=0)


def broadcast(shard, axis, root):
    return lax.dynamic_index_in_dim(lax.all_gather(shard, axis), root, 0, keepdims=False)


def local(activations, out_grads, basis, first_moment, second_moment, reward_codes, token_ids):
    data_count = lax.axis_size("dp")
    tensor_count = lax.axis_size("tensor")
    partial_value = jnp.dot(activations, basis, preferred_element_type=jnp.float32)
    projected = total_of(partial_value.astype(jnp.bfloat16), "tensor")
    unmasked = (token_ids != pad_token).astype(jnp.float32)
    weights = unmasked * jnp.exp(reward_temp * reward_codes.astype(jnp.float32))
    local_total = jnp.sum(weights)
    weighted = (weights[:, None] * projected).astype(jnp.bfloat16)
    raw_grad = lax.dot_general(
        weighted, out_grads, (((0,), (0,)), ((), ())), preferred_element_type=jnp.float32
    )
    normalizer = of_everyone(local_total, "dp")
    grad_rows = sum_at_owner(raw_grad.astype(jnp.bfloat16), "dp", 0)
    token_count = activations.shape[0] * data_count
    gradient = grad_rows * (token_count / normalizer)
    new_first = beta_one * first_moment + (1.0 - beta_one) * gradient
    new_second = beta_two * second_moment + (1.0 - beta_two) * gradient * gradient
    bias_one = 1.0 - beta_one**ADAM_STEP
    bias_two = 1.0 - beta_two**ADAM_STEP
    update = (new_first / bias_one / (jnp.sqrt(new_second / bias_two) + adam_eps)).astype(
        jnp.bfloat16
    )
    data_index = lax.axis_index("dp")
    owner_index = data_index * tensor_count // data_count
    owner_rows = broadcast(basis, "tensor", owner_index)
    summed = jnp.dot(
        owner_rows,
        lax.all_gather(update, "dp", axis=0, tiled=True),
        preferred_element_type=jnp.float32,
    )
    return (new_first, new_second, summed.astype(jnp.bfloat16))


def solution(mesh):
    return jax.shard_map(
        local,
        mesh=mesh,
        in_specs=(
            P("dp", "tensor"),
            P("dp", "tensor"),
            P("tensor", None),
            P("dp", "tensor"),
            P("dp", "tensor"),
            P("dp"),
            P("dp"),
        ),
        out_specs=(P("dp", "tensor"), P("dp", "tensor"), P("dp", "tensor")),
        check_vma=False,
    )
```

profile of v0, /device:TPU:1, one launch (start us, length us, event | category | flops | bytes accessed | tf_op | source)
XLA Modules:
  0.0 148.8 jit_solution(3367582259047807124)
XLA Ops:
  7.2 0.0 copy-start
  7.2 0.0 all-gather.3.cloned.1.call-start
  7.2 0.7 all-gather.3.cloned.1.call-update
  7.9 0.9 copy-done
  8.8 1.7 %convolution_convert_fusion = bf16[2304,256]{1,0:T(8,128)(2,1)S(1)} fusion(bf16[2304,512]{1,0:T(8,128)(2,1)S(1)} %copy-done, bf16[512,256]{1,0:T(8,128)(2,1)} %param.9), kind=kOutput, calls=%fused_computation | convolution fusion | flops 604569600 | bytes 3801088 | tf_op jit(solution)/shard_map/dot_general | solution.py:65
  10.6 26.5 %all_to_all.21 = bf16[16,144,256]{2,1,0:T(8,128)(2,1)S(1)} all-to-all(bf16[16,144,256]{2,1,0:T(8,128)(2,1)S(1)} %bitcast.14), channel_id=1, replica_groups=mesh['dp'=16,'tensor'=16] {'tensor'}, dimensions={0} | all-to-all | bytes 2359296 | tf_op jit(solution)/shard_map/all_to_all | solution.py:43
  37.1 0.8 reduce_sum.39
  37.9 2.0 %broadcast_in_dim.4 = bf16[16,144,256]{2,1,0:T(8,128)(2,1)} broadcast(bf16[144,256]{1,0:T(8,128)(2,1)} %reduce_sum.39), dimensions={1,2} | broadcast | bytes 1253376 | tf_op jit(solution)/shard_map/broadcast_in_dim | solution.py:28
  39.9 3.7 %all-to-all-start.1 = ((bf16[16,144,256]{2,1,0:T(8,128)(2,1)}), bf16[16,144,256]{2,1,0:T(8,128)(2,1)S(1)}, u32[]{:S(2)}, u32[]{:S(2)}) async-start(bf16[16,144,256]{2,1,0:T(8,128)(2,1)} %broadcast_in_dim.4), calls=%async_computation.1 | async-start | bytes 2359296 | tf_op jit(solution)/shard_map/all_to_all | solution.py:27
  43.6 1.3 fusion.8
  44.9 14.6 %all-to-all-done.1 = bf16[16,144,256]{2,1,0:T(8,128)(2,1)S(1)} async-done(((bf16[16,144,256]{2,1,0:T(8,128)(2,1)}), bf16[16,144,256]{2,1,0:T(8,128)(2,1)S(1)}, u32[]{:S(2)}, u32[]{:S(2)}) %all-to-all-start.1) | async-done | bytes 1179680 | tf_op jit(solution)/shard_map/all_to_all | solution.py:27
  59.6 1.2 broadcast_in_dim.5
  60.8 21.0 %all-to-all-start.3 = ((f32[16,1,1]{2,1,0:T(1,128)}), f32[16,1,1]{2,1,0:T(1,128)}, u32[]{:S(2)}, u32[]{:S(2)}) async-start(f32[16,1,1]{2,1,0:T(1,128)} %broadcast_in_dim.5), calls=%async_computation.3 | async-start | bytes 16384 | tf_op jit(solution)/shard_map/all_to_all | solution.py:27
  81.9 6.7 %convolution_convert_fusion.2 = bf16[256,1792]{1,0:T(8,128)(2,1)} fusion(bf16[2304,1792]{1,0:T(8,128)(2,1)} %param.8, bf16[2304,256]{1,0:T(8,128)(2,1)S(1)} %bitcast.12, f32[2304]{0:T(1024)S(1)} %get-tuple-element.7), kind=kOutput, calls=%fused_computation.2 | convolution fusion | flops 2116157440 | bytes 10363904 | tf_op jit(solution)/shard_map/dot_general | solution.py:71
  88.6 0.0 copy-start.1
  88.6 0.0 copy-start.2
  88.6 0.3 all-to-all-done.3
  88.9 7.0 %all-to-all-start.2 = ((bf16[16,16,1792]{2,1,0:T(8,128)(2,1)}), bf16[16,16,1792]{2,1,0:T(8,128)(2,1)S(1)}, u32[]{:S(2)}, u32[]{:S(2)}) async-start(bf16[16,16,1792]{2,1,0:T(8,128)(2,1)} %bitcast.13), calls=%async_computation.2 | async-start | bytes 1835008 | tf_op jit(solution)/shard_map/all_to_all | solution.py:43
  96.0 1.3 reduce_sum.42
  98.0 23.3 %all-to-all-done.2 = bf16[16,16,1792]{2,1,0:T(8,128)(2,1)S(1)} async-done(((bf16[16,16,1792]{2,1,0:T(8,128)(2,1)}), bf16[16,16,1792]{2,1,0:T(8,128)(2,1)S(1)}, u32[]{:S(2)}, u32[]{:S(2)}) %all-to-all-start.2) | async-done | bytes 917536 | tf_op jit(solution)/shard_map/all_to_all | solution.py:43
  121.2 0.1 convert_reduce_fusion
  121.4 0.0 copy-done.1
  121.4 0.0 copy-done.2
  121.4 0.8 divide_convert_fusion
  122.2 17.0 %all_gather.11 = bf16[256,1792]{1,0:T(8,128)(2,1)S(1)} all-gather(bf16[16,1792]{1,0:T(8,128)(2,1)S(1)} %get-tuple-element.3), channel_id=1, replica_groups=mesh['dp'=16,'tensor'=16] {'dp'}, dimensions={0}, use_global_device_ids=true | all-gather | bytes 974848 | tf_op jit(solution)/shard_map/all_gather | solution.py:90
  139.1 0.0 all-gather.3.cloned.1.call-done
  139.1 2.8 %convolution_convert_fusion.1 = bf16[512,1792]{1,0:T(8,128)(2,1)} fusion(bf16[256,1792]{1,0:T(8,128)(2,1)S(1)} %all_gather.11, bf16[16,512,256]{2,1,0:T(8,128)(2,1)} %bitcast.15, s32[]{:T(128)S(6)} %select_n.10), kind=kOutput, calls=%fused_computation.1 | convolution fusion | flops 470679552 | bytes 3014660 | tf_op jit(solution)/shard_map/dot_general | solution.py:88
Async XLA Ops:
  7.2 1.7 %copy-start = (bf16[2304,512]{1,0:T(8,128)(2,1)S(1)}, bf16[2304,512]{1,0:T(8,128)(2,1)}, u32[]{:S(2)}) copy-start(bf16[2304,512]{1,0:T(8,128)(2,1)} %param.7) | copy-start | bytes 7077892
  7.2 132.0 %all-gather.3.cloned.1.call-start = ((), (), s32[]{:S(2)}) async-start(), calls=%async_computation.4 | async-start | bytes 4456448 | tf_op jit(solution)/shard_map/all_gather | solution.py:59
  39.9 19.7 %all-to-all-start.1 = ((bf16[16,144,256]{2,1,0:T(8,128)(2,1)}), bf16[16,144,256]{2,1,0:T(8,128)(2,1)S(1)}, u32[]{:S(2)}, u32[]{:S(2)}) async-start(bf16[16,144,256]{2,1,0:T(8,128)(2,1)} %broadcast_in_dim.4), calls=%async_computation.1 | async-start | bytes 2359296 | tf_op jit(solution)/shard_map/all_to_all | solution.py:27
  60.8 28.1 %all-to-all-start.3 = ((f32[16,1,1]{2,1,0:T(1,128)}), f32[16,1,1]{2,1,0:T(1,128)}, u32[]{:S(2)}, u32[]{:S(2)}) async-start(f32[16,1,1]{2,1,0:T(1,128)} %broadcast_in_dim.5), calls=%async_computation.3 | async-start | bytes 16384 | tf_op jit(solution)/shard_map/all_to_all | solution.py:27
  88.6 32.8 %copy-start.1 = (f32[16,1792]{1,0:T(8,128)S(1)}, f32[16,1792]{1,0:T(8,128)}, u32[]{:S(2)}) copy-start(f32[16,1792]{1,0:T(8,128)} %param.11) | copy-start | bytes 344068
  88.6 32.8 %copy-start.2 = (f32[16,1792]{1,0:T(8,128)S(1)}, f32[16,1792]{1,0:T(8,128)}, u32[]{:S(2)}) copy-start(f32[16,1792]{1,0:T(8,128)} %param.10) | copy-start | bytes 344068
  88.9 32.3 %all-to-all-start.2 = ((bf16[16,16,1792]{2,1,0:T(8,128)(2,1)}), bf16[16,16,1792]{2,1,0:T(8,128)(2,1)S(1)}, u32[]{:S(2)}, u32[]{:S(2)}) async-start(bf16[16,16,1792]{2,1,0:T(8,128)(2,1)} %bitcast.13), calls=%async_computation.2 | async-start | bytes 1835008 | tf_op jit(solution)/shard_map/all_to_all | solution.py:43
Sparse Core Ops, SparseCore 0:
  10.4 67.8 all-gather.2
where the time goes:
time: 149 us
  blocking collectives  43.5 us (29%)
  waiting for transfers between devices  38.9 us (26%)
  starting transfers between devices  31.8 us (21%)
  between operations  14.8 us (10%)
  matrix products  11.3 us (8%)
  other arithmetic  4.34 us (3%)
  local copies, waits for them, and re-layouts  4.16 us (3%)
    all_to_all x1, blocking collectives, sum_at_owner(): lax.all_to_all(parts, axis, split_axis=0, concat_axis=0, tiled=True)  26.5 us
    all_to_all x2, starting transfers between devices, sent_to_all(): lax.all_to_all(jnp.broadcast_to(shard[None], (size, *shard.shape)), axis,...  24.7 us
    all_to_all x1, waiting for transfers between devices, sum_at_owner(): lax.all_to_all(parts, axis, split_axis=0, concat_axis=0, tiled=True)  23.3 us
    all_gather x1, blocking collectives, local(): lax.all_gather(update, 'dp', axis=0, tiled=True)  17 us
    all_to_all x2, waiting for transfers between devices, sent_to_all(): lax.all_to_all(jnp.broadcast_to(shard[None], (size, *shard.shape)), axis,...  15 us
    all_to_all x1, starting transfers between devices, sum_at_owner(): lax.all_to_all(parts, axis, split_axis=0, concat_axis=0, tiled=True)  7.04 us
    dot_general x1, matrix products, local(): lax.dot_general(weighted, out_grads, (((0,), (0,)), ((), ())), preferred_...  6.72 us
    broadcast_in_dim x2, local copies, waits for them, and re-layouts, sent_to_all(): jnp.broadcast_to(shard[None], (size, *shard.shape))  3.22 us
  transfers between devices with their start and end apart: 4, of which 3 were waited for; matrix products, arithmetic and copies ran while one was open for 11% of the time, Pallas kernels for 0%

commit v1 on v0

--- a/solution.py
+++ b/solution.py
@@ -9,6 +9,19 @@
 beta_one = 0.9
 beta_two = 0.999
 adam_eps = 1e-08
+
+
+def gather_around(value, axis, dim):
+    ways = lax.axis_size(axis)
+    up = [(d, (d + 1) % ways) for d in range(ways)]
+    down = [(d, (d - 1) % ways) for d in range(ways)]
+    earlier, later = ([value], [value])
+    for _ in range(ways // 2):
+        earlier.append(lax.ppermute(earlier[-1], axis, up))
+    for _ in range((ways - 1) // 2):
+        later.append(lax.ppermute(later[-1], axis, down))
+    line = jnp.concatenate([*earlier[::-1], *later[1:]], axis=dim)
+    return jnp.roll(line, (lax.axis_index(axis) - ways // 2) * value.shape[dim], axis=dim)
 
 
 def filled_up(lines, size):
@@ -85,11 +98,7 @@
     data_index = lax.axis_index("dp")
     owner_index = data_index * tensor_count // data_count
     owner_rows = broadcast(basis, "tensor", owner_index)
-    summed = jnp.dot(
-        owner_rows,
-        lax.all_gather(update, "dp", axis=0, tiled=True),
-        preferred_element_type=jnp.float32,
-    )
+    summed = jnp.dot(owner_rows, gather_around(update, "dp", 0), preferred_element_type=jnp.float32)
     return (new_first, new_second, summed.astype(jnp.bfloat16))
 
 

time: 149 us -> 177 us (1.19); the launches traced: 149 us -> 175 us
  local copies, waits for them, and re-layouts: 4.16 us -> 24.9 us
  blocking collectives: 43.5 us -> 24.8 us
  starting transfers between devices: 31.8 us -> 47.8 us
  waiting for transfers between devices: 38.9 us -> 46.8 us
    ppermute x0 -> x15, starting transfers between devices: none -> 24.9 us  [the longest x7 17.4 us: gather_around(): later.append(lax.ppermute(later[-1], axis, down))]
    unnamed x6 -> x37, local copies, waits for them, and re-layouts: 0.94 us -> 21 us
    all_gather x1 -> x0, blocking collectives: 17 us -> none  [local(): lax.all_gather(update, 'dp', axis=0, tiled=True)]
    all_to_all x2, starting transfers between devices: 24.7 us -> 15.7 us  [sent_to_all(): lax.all_to_all(jnp.broadcast_to(shard[None], (size, *shard.shape)), axis,...]
    ppermute x0 -> x15, waiting for transfers between devices: none -> 8.43 us  [the longest x8 5.06 us: gather_around(): earlier.append(lax.ppermute(earlier[-1], axis, up))]
  transfers between devices with their start and end apart: 4 -> 19, of which waited for: 3 -> 15; matrix products, arithmetic and copies ran while one was open for 11% -> 17% of each run, Pallas kernels for 0% -> 0%
where the time goes in v1:
time: 177 us; the launch traced here: 175 us
  starting transfers between devices  47.8 us (27%)
  waiting for transfers between devices  46.8 us (26%)
  local copies, waits for them, and re-layouts  24.9 us (14%)
  blocking collectives  24.8 us (14%)
  between operations  14.8 us (8%)
  matrix products  11.6 us (7%)
  other arithmetic  4.35 us (2%)
    all_to_all x1, blocking collectives, sum_at_owner(): lax.all_to_all(parts, axis, split_axis=0, concat_axis=0, tiled=True)  24.8 us
    all_to_all x1, waiting for transfers between devices, sum_at_owner(): lax.all_to_all(parts, axis, split_axis=0, concat_axis=0, tiled=True)  22.6 us
    unnamed x37, local copies, waits for them, and re-layouts  21 us
    ppermute x7, starting transfers between devices, gather_around(): later.append(lax.ppermute(later[-1], axis, down))  17.4 us
    all_to_all x2, starting transfers between devices, sent_to_all(): lax.all_to_all(jnp.broadcast_to(shard[None], (size, *shard.shape)), axis,...  15.7 us
    all_to_all x2, waiting for transfers between devices, sent_to_all(): lax.all_to_all(jnp.broadcast_to(shard[None], (size, *shard.shape)), axis,...  15.2 us
    ppermute x8, starting transfers between devices, gather_around(): earlier.append(lax.ppermute(earlier[-1], axis, up))  7.51 us
    all_to_all x1, starting transfers between devices, sum_at_owner(): lax.all_to_all(parts, axis, split_axis=0, concat_axis=0, tiled=True)  7.19 us
  transfers between devices with their start and end apart: 19, of which 15 were waited for; matrix products, arithmetic and copies ran while one was open for 17% of the time, Pallas kernels for 0%

profile of v1, /device:TPU:1, one launch (start us, length us, event | category | flops | bytes accessed | tf_op | source)
XLA Modules:
  0.0 175.0 jit_solution(14265469233357354165)
XLA Ops:
  7.2 1.7 copy-done
  8.8 1.7 convolution_convert_fusion
  10.6 24.8 %all_to_all.21 = bf16[16,144,256]{2,1,0:T(8,128)(2,1)S(1)} all-to-all(bf16[16,144,256]{2,1,0:T(8,128)(2,1)S(1)} %bitcast.13), channel_id=1, replica_groups=mesh['dp'=16,'tensor'=16] {'tensor'}, dimensions={0} | all-to-all | bytes 2359296 | tf_op jit(solution)/shard_map/all_to_all | solution.py:56
  35.4 0.8 reduce_sum.39
  36.2 2.0 %broadcast_in_dim.4 = bf16[16,144,256]{2,1,0:T(8,128)(2,1)} broadcast(bf16[144,256]{1,0:T(8,128)(2,1)} %reduce_sum.39), dimensions={1,2} | broadcast | bytes 1253376 | tf_op jit(solution)/shard_map/broadcast_in_dim | solution.py:41
  38.1 3.7 %all-to-all-start.1 = ((bf16[16,144,256]{2,1,0:T(8,128)(2,1)}), bf16[16,144,256]{2,1,0:T(8,128)(2,1)S(1)}, u32[]{:S(2)}, u32[]{:S(2)}) async-start(bf16[16,144,256]{2,1,0:T(8,128)(2,1)} %broadcast_in_dim.4), calls=%async_computation.1 | async-start | bytes 2359296 | tf_op jit(solution)/shard_map/all_to_all | solution.py:40
  41.9 1.3 fusion.9
  43.2 15.0 %all-to-all-done.1 = bf16[16,144,256]{2,1,0:T(8,128)(2,1)S(1)} async-done(((bf16[16,144,256]{2,1,0:T(8,128)(2,1)}), bf16[16,144,256]{2,1,0:T(8,128)(2,1)S(1)}, u32[]{:S(2)}, u32[]{:S(2)}) %all-to-all-start.1) | async-done | bytes 1179680 | tf_op jit(solution)/shard_map/all_to_all | solution.py:40
  58.2 1.2 broadcast_in_dim.5
  59.4 12.0 %all-to-all-start.3 = ((f32[16,1,1]{2,1,0:T(1,128)}), f32[16,1,1]{2,1,0:T(1,128)}, u32[]{:S(2)}, u32[]{:S(2)}) async-start(f32[16,1,1]{2,1,0:T(1,128)} %broadcast_in_dim.5), calls=%async_computation.3 | async-start | bytes 16384 | tf_op jit(solution)/shard_map/all_to_all | solution.py:40
  71.4 6.7 %convolution_convert_fusion.2 = bf16[256,1792]{1,0:T(8,128)(2,1)} fusion(bf16[2304,1792]{1,0:T(8,128)(2,1)} %param.8, bf16[2304,256]{1,0:T(8,128)(2,1)S(1)} %bitcast.11, f32[2304]{0:T(1024)S(1)} %get-tuple-element.7), kind=kOutput, calls=%fused_computation.2 | convolution fusion | flops 2116157440 | bytes 10363904 | tf_op jit(solution)/shard_map/dot_general | solution.py:84
  78.3 7.2 %all-to-all-start.2 = ((bf16[16,16,1792]{2,1,0:T(8,128)(2,1)}), bf16[16,16,1792]{2,1,0:T(8,128)(2,1)S(1)}, u32[]{:S(2)}, u32[]{:S(2)}) async-start(bf16[16,16,1792]{2,1,0:T(8,128)(2,1)} %bitcast.12), calls=%async_computation.2 | async-start | bytes 1835008 | tf_op jit(solution)/shard_map/all_to_all | solution.py:56
  85.5 0.7 all-gather.3.cloned.1.call-update
  86.2 1.3 reduce_sum.42
  88.2 22.6 %all-to-all-done.2 = bf16[16,16,1792]{2,1,0:T(8,128)(2,1)S(1)} async-done(((bf16[16,16,1792]{2,1,0:T(8,128)(2,1)}), bf16[16,16,1792]{2,1,0:T(8,128)(2,1)S(1)}, u32[]{:S(2)}, u32[]{:S(2)}) %all-to-all-start.2) | async-done | bytes 917536 | tf_op jit(solution)/shard_map/all_to_all | solution.py:56
  110.9 0.8 divide_convert_fusion
  111.7 1.3 collective-permute-done
  113.0 2.3 %collective-permute-start.1 = (bf16[16,1792]{1,0:T(8,128)(2,1)S(1)}, bf16[16,1792]{1,0:T(8,128)(2,1)S(1)}, u32[]{:S(2)}, u32[]{:S(2)}) collective-permute-start(bf16[16,1792]{1,0:T(8,128)(2,1)S(1)} %collective-permute-done), channel_id=1, source_target_pairs={{0,16},{16,32},{32,48},{48,64},{64,80},{80,96},{96,112},{112,128},... | collective-permute-start | bytes 172040 | tf_op jit(solution)/shard_map/ppermute | solution.py:20
  115.3 1.3 collective-permute-done.1
  116.6 2.3 %collective-permute-start.2 = (bf16[16,1792]{1,0:T(8,128)(2,1)S(1)}, bf16[16,1792]{1,0:T(8,128)(2,1)S(1)}, u32[]{:S(2)}, u32[]{:S(2)}) collective-permute-start(bf16[16,1792]{1,0:T(8,128)(2,1)S(1)} %collective-permute-done.1), channel_id=1, source_target_pairs={{0,16},{16,32},{32,48},{48,64},{64,80},{80,96},{96,112},{112,128},... | collective-permute-start | bytes 172040 | tf_op jit(solution)/shard_map/ppermute | solution.py:20
  119.8 0.7 collective-permute-done.2
  120.5 2.0 %collective-permute-start.3 = (bf16[16,1792]{1,0:T(8,128)(2,1)S(1)}, bf16[16,1792]{1,0:T(8,128)(2,1)S(1)}, u32[]{:S(2)}, u32[]{:S(2)}) collective-permute-start(bf16[16,1792]{1,0:T(8,128)(2,1)S(1)} %collective-permute-done.2), channel_id=1, source_target_pairs={{0,16},{16,32},{32,48},{48,64},{64,80},{80,96},{96,112},{112,128},... | collective-permute-start | bytes 172040 | tf_op jit(solution)/shard_map/ppermute | solution.py:20
  122.8 1.8 %collective-permute-start.10 = (bf16[16,1792]{1,0:T(8,128)(2,1)S(1)}, bf16[16,1792]{1,0:T(8,128)(2,1)S(1)}, u32[]{:S(2)}, u32[]{:S(2)}) collective-permute-start(bf16[16,1792]{1,0:T(8,128)(2,1)S(1)} %collective-permute-done.9), channel_id=1, source_target_pairs={{0,240},{16,0},{32,16},{48,32},{64,48},{80,64},{96,80},{112,96},{1... | collective-permute-start | bytes 172040 | tf_op jit(solution)/shard_map/ppermute | solution.py:22
  124.6 0.7 collective-permute-done.3
  125.3 0.8 collective-permute-start.4
  126.1 0.7 collective-permute-done.10
  126.8 2.6 %collective-permute-start.11 = (bf16[16,1792]{1,0:T(8,128)(2,1)S(1)}, bf16[16,1792]{1,0:T(8,128)(2,1)S(1)}, u32[]{:S(2)}, u32[]{:S(2)}) collective-permute-start(bf16[16,1792]{1,0:T(8,128)(2,1)S(1)} %collective-permute-done.10), channel_id=1, source_target_pairs={{0,240},{16,0},{32,16},{48,32},{64,48},{80,64},{96,80},{112,96},{1... | collective-permute-start | bytes 172040 | tf_op jit(solution)/shard_map/ppermute | solution.py:22
  129.4 0.7 collective-permute-done.4
  130.1 0.7 collective-permute-done.11
  130.8 3.8 %collective-permute-start.12 = (bf16[16,1792]{1,0:T(8,128)(2,1)S(1)}, bf16[16,1792]{1,0:T(8,128)(2,1)S(1)}, u32[]{:S(2)}, u32[]{:S(2)}) collective-permute-start(bf16[16,1792]{1,0:T(8,128)(2,1)S(1)} %collective-permute-done.11), channel_id=1, source_target_pairs={{0,240},{16,0},{32,16},{48,32},{64,48},{80,64},{96,80},{112,96},{1... | collective-permute-start | bytes 172040 | tf_op jit(solution)/shard_map/ppermute | solution.py:22
  135.5 4.3 %collective-permute-start.13 = (bf16[16,1792]{1,0:T(8,128)(2,1)S(1)}, bf16[16,1792]{1,0:T(8,128)(2,1)S(1)}, u32[]{:S(2)}, u32[]{:S(2)}) collective-permute-start(bf16[16,1792]{1,0:T(8,128)(2,1)S(1)} %collective-permute-done.12), channel_id=1, source_target_pairs={{0,240},{16,0},{32,16},{48,32},{64,48},{80,64},{96,80},{112,96},{1... | collective-permute-start | bytes 172040 | tf_op jit(solution)/shard_map/ppermute | solution.py:22
  139.8 0.9 collective-permute-done.13
  140.7 4.3 %collective-permute-start.14 = (bf16[16,1792]{1,0:T(8,128)(2,1)S(1)}, bf16[16,1792]{1,0:T(8,128)(2,1)S(1)}, u32[]{:S(2)}, u32[]{:S(2)}) collective-permute-start(bf16[16,1792]{1,0:T(8,128)(2,1)S(1)} %collective-permute-done.13), channel_id=1, source_target_pairs={{0,240},{16,0},{32,16},{48,32},{64,48},{80,64},{96,80},{112,96},{1... | collective-permute-start | bytes 172040 | tf_op jit(solution)/shard_map/ppermute | solution.py:22
  145.0 0.6 constant_dynamic-update-slice_fusion.31
  145.7 0.6 constant_dynamic-update-slice_fusion.30
  146.3 0.6 constant_dynamic-update-slice_fusion.29
  146.9 0.6 constant_dynamic-update-slice_fusion.28
  147.5 0.6 constant_dynamic-update-slice_fusion.27
  148.1 0.6 constant_dynamic-update-slice_fusion.26
  148.8 0.6 constant_dynamic-update-slice_fusion.25
  149.4 0.6 constant_dynamic-update-slice_fusion.24
  150.0 0.6 constant_dynamic-update-slice_fusion.23
  150.6 0.6 constant_dynamic-update-slice_fusion.22
  151.3 0.6 constant_dynamic-update-slice_fusion.21
  151.9 0.6 constant_dynamic-update-slice_fusion.20
  153.1 0.6 constant_dynamic-update-slice_fusion.18
  153.8 0.6 constant_dynamic-update-slice_fusion.17
  154.4 0.6 constant_dynamic-update-slice_fusion.16
  155.6 0.6 constant_dynamic-update-slice_fusion.14
  156.3 0.6 constant_dynamic-update-slice_fusion.13
  156.9 0.6 constant_dynamic-update-slice_fusion.12
  157.5 0.6 constant_dynamic-update-slice_fusion.11
  158.1 0.6 constant_dynamic-update-slice_fusion.10
  158.8 0.6 constant_dynamic-update-slice_fusion.9
  159.4 0.6 constant_dynamic-update-slice_fusion.8
  160.0 0.6 constant_dynamic-update-slice_fusion.7
  160.6 0.6 constant_dynamic-update-slice_fusion.6
  161.3 0.6 constant_dynamic-update-slice_fusion.5
  161.9 0.6 constant_dynamic-update-slice_fusion.4
  162.5 0.6 constant_dynamic-update-slice_fusion.3
  163.1 0.6 constant_dynamic-update-slice_fusion.2
  163.8 0.6 constant_dynamic-update-slice_fusion.1
  164.4 0.6 constant_dynamic-update-slice_fusion
  165.0 3.1 %convolution_convert_fusion.1 = bf16[512,1792]{1,0:T(8,128)(2,1)} fusion(bf16[512,1792]{1,0:T(8,128)(2,1)} %constant_dynamic-update-slice_fusion, s32[]{:T(128)S(6)} %select_n.24, bf16[16,512,256]{2,1,0:T(8,128)(2,1)} %bitcast.14, s32[]{:T(128)S(6)} %select_n.22), kind=kOutput, calls=%fused_computation.1 | convolution fusion | flops 470679552 | bytes 3014664 | tf_op jit(solution)/shard_map/dot_general | solution.py:101
  (24 shorter events, 3.7 us)
Async XLA Ops:
  7.2 1.7 copy-start
  38.1 20.1 %all-to-all-start.1 = ((bf16[16,144,256]{2,1,0:T(8,128)(2,1)}), bf16[16,144,256]{2,1,0:T(8,128)(2,1)S(1)}, u32[]{:S(2)}, u32[]{:S(2)}) async-start(bf16[16,144,256]{2,1,0:T(8,128)(2,1)} %broadcast_in_dim.4), calls=%async_computation.1 | async-start | bytes 2359296 | tf_op jit(solution)/shard_map/all_to_all | solution.py:40
  59.4 18.9 %all-to-all-start.3 = ((f32[16,1,1]{2,1,0:T(1,128)}), f32[16,1,1]{2,1,0:T(1,128)}, u32[]{:S(2)}, u32[]{:S(2)}) async-start(f32[16,1,1]{2,1,0:T(1,128)} %broadcast_in_dim.5), calls=%async_computation.3 | async-start | bytes 16384 | tf_op jit(solution)/shard_map/all_to_all | solution.py:40
  78.1 32.8 %copy-start.1 = (f32[16,1792]{1,0:T(8,128)S(1)}, f32[16,1792]{1,0:T(8,128)}, u32[]{:S(2)}) copy-start(f32[16,1792]{1,0:T(8,128)} %param.11) | copy-start | bytes 344068
  78.1 32.8 %copy-start.2 = (f32[16,1792]{1,0:T(8,128)S(1)}, f32[16,1792]{1,0:T(8,128)}, u32[]{:S(2)}) copy-start(f32[16,1792]{1,0:T(8,128)} %param.10) | copy-start | bytes 344068
  78.3 32.5 %all-to-all-start.2 = ((bf16[16,16,1792]{2,1,0:T(8,128)(2,1)}), bf16[16,16,1792]{2,1,0:T(8,128)(2,1)S(1)}, u32[]{:S(2)}, u32[]{:S(2)}) async-start(bf16[16,16,1792]{2,1,0:T(8,128)(2,1)} %bitcast.12), calls=%async_computation.2 | async-start | bytes 1835008 | tf_op jit(solution)/shard_map/all_to_all | solution.py:56
  85.5 79.5 %all-gather.3.cloned.1.call-start = ((), (), s32[]{:S(2)}) async-start(), calls=%async_computation.4 | async-start | bytes 4456448 | tf_op jit(solution)/shard_map/all_gather | solution.py:72
  111.7 1.3 collective-permute-start
  113.0 3.6 %collective-permute-start.1 = (bf16[16,1792]{1,0:T(8,128)(2,1)S(1)}, bf16[16,1792]{1,0:T(8,128)(2,1)S(1)}, u32[]{:S(2)}, u32[]{:S(2)}) collective-permute-start(bf16[16,1792]{1,0:T(8,128)(2,1)S(1)} %collective-permute-done), channel_id=1, source_target_pairs={{0,16},{16,32},{32,48},{48,64},{64,80},{80,96},{96,112},{112,128},... | collective-permute-start | bytes 172040 | tf_op jit(solution)/shard_map/ppermute | solution.py:20
  115.3 3.9 %collective-permute-start.8 = (bf16[16,1792]{1,0:T(8,128)(2,1)S(1)}, bf16[16,1792]{1,0:T(8,128)(2,1)S(1)}, u32[]{:S(2)}, u32[]{:S(2)}) collective-permute-start(bf16[16,1792]{1,0:T(8,128)(2,1)S(1)} %get-tuple-element.3), channel_id=1, source_target_pairs={{0,240},{16,0},{32,16},{48,32},{64,48},{80,64},{96,80},{112,96},{1... | collective-permute-start | bytes 172040 | tf_op jit(solution)/shard_map/ppermute | solution.py:22
  116.6 3.9 %collective-permute-start.2 = (bf16[16,1792]{1,0:T(8,128)(2,1)S(1)}, bf16[16,1792]{1,0:T(8,128)(2,1)S(1)}, u32[]{:S(2)}, u32[]{:S(2)}) collective-permute-start(bf16[16,1792]{1,0:T(8,128)(2,1)S(1)} %collective-permute-done.1), channel_id=1, source_target_pairs={{0,16},{16,32},{32,48},{48,64},{64,80},{80,96},{96,112},{112,128},... | collective-permute-start | bytes 172040 | tf_op jit(solution)/shard_map/ppermute | solution.py:20
  119.2 3.6 %collective-permute-start.9 = (bf16[16,1792]{1,0:T(8,128)(2,1)S(1)}, bf16[16,1792]{1,0:T(8,128)(2,1)S(1)}, u32[]{:S(2)}, u32[]{:S(2)}) collective-permute-start(bf16[16,1792]{1,0:T(8,128)(2,1)S(1)} %collective-permute-done.8), channel_id=1, source_target_pairs={{0,240},{16,0},{32,16},{48,32},{64,48},{80,64},{96,80},{112,96},{1... | collective-permute-start | bytes 172040 | tf_op jit(solution)/shard_map/ppermute | solution.py:22
  120.5 4.8 %collective-permute-start.3 = (bf16[16,1792]{1,0:T(8,128)(2,1)S(1)}, bf16[16,1792]{1,0:T(8,128)(2,1)S(1)}, u32[]{:S(2)}, u32[]{:S(2)}) collective-permute-start(bf16[16,1792]{1,0:T(8,128)(2,1)S(1)} %collective-permute-done.2), channel_id=1, source_target_pairs={{0,16},{16,32},{32,48},{48,64},{64,80},{80,96},{96,112},{112,128},... | collective-permute-start | bytes 172040 | tf_op jit(solution)/shard_map/ppermute | solution.py:20
  122.8 4.0 %collective-permute-start.10 = (bf16[16,1792]{1,0:T(8,128)(2,1)S(1)}, bf16[16,1792]{1,0:T(8,128)(2,1)S(1)}, u32[]{:S(2)}, u32[]{:S(2)}) collective-permute-start(bf16[16,1792]{1,0:T(8,128)(2,1)S(1)} %collective-permute-done.9), channel_id=1, source_target_pairs={{0,240},{16,0},{32,16},{48,32},{64,48},{80,64},{96,80},{112,96},{1... | collective-permute-start | bytes 172040 | tf_op jit(solution)/shard_map/ppermute | solution.py:22
  125.3 4.8 %collective-permute-start.4 = (bf16[16,1792]{1,0:T(8,128)(2,1)S(1)}, bf16[16,1792]{1,0:T(8,128)(2,1)S(1)}, u32[]{:S(2)}, u32[]{:S(2)}) collective-permute-start(bf16[16,1792]{1,0:T(8,128)(2,1)S(1)} %collective-permute-done.3), channel_id=1, source_target_pairs={{0,16},{16,32},{32,48},{48,64},{64,80},{80,96},{96,112},{112,128},... | collective-permute-start | bytes 172040 | tf_op jit(solution)/shard_map/ppermute | solution.py:20
  126.8 4.0 %collective-permute-start.11 = (bf16[16,1792]{1,0:T(8,128)(2,1)S(1)}, bf16[16,1792]{1,0:T(8,128)(2,1)S(1)}, u32[]{:S(2)}, u32[]{:S(2)}) collective-permute-start(bf16[16,1792]{1,0:T(8,128)(2,1)S(1)} %collective-permute-done.10), channel_id=1, source_target_pairs={{0,240},{16,0},{32,16},{48,32},{64,48},{80,64},{96,80},{112,96},{1... | collective-permute-start | bytes 172040 | tf_op jit(solution)/shard_map/ppermute | solution.py:22
  130.1 4.8 %collective-permute-start.5 = (bf16[16,1792]{1,0:T(8,128)(2,1)S(1)}, bf16[16,1792]{1,0:T(8,128)(2,1)S(1)}, u32[]{:S(2)}, u32[]{:S(2)}) collective-permute-start(bf16[16,1792]{1,0:T(8,128)(2,1)S(1)} %collective-permute-done.4), channel_id=1, source_target_pairs={{0,16},{16,32},{32,48},{48,64},{64,80},{80,96},{96,112},{112,128},... | collective-permute-start | bytes 172040 | tf_op jit(solution)/shard_map/ppermute | solution.py:20
  130.8 4.7 %collective-permute-start.12 = (bf16[16,1792]{1,0:T(8,128)(2,1)S(1)}, bf16[16,1792]{1,0:T(8,128)(2,1)S(1)}, u32[]{:S(2)}, u32[]{:S(2)}) collective-permute-start(bf16[16,1792]{1,0:T(8,128)(2,1)S(1)} %collective-permute-done.11), channel_id=1, source_target_pairs={{0,240},{16,0},{32,16},{48,32},{64,48},{80,64},{96,80},{112,96},{1... | collective-permute-start | bytes 172040 | tf_op jit(solution)/shard_map/ppermute | solution.py:22
  135.0 4.9 %collective-permute-start.6 = (bf16[16,1792]{1,0:T(8,128)(2,1)S(1)}, bf16[16,1792]{1,0:T(8,128)(2,1)S(1)}, u32[]{:S(2)}, u32[]{:S(2)}) collective-permute-start(bf16[16,1792]{1,0:T(8,128)(2,1)S(1)} %collective-permute-done.5), channel_id=1, source_target_pairs={{0,16},{16,32},{32,48},{48,64},{64,80},{80,96},{96,112},{112,128},... | collective-permute-start | bytes 172040 | tf_op jit(solution)/shard_map/ppermute | solution.py:20
  135.5 5.2 %collective-permute-start.13 = (bf16[16,1792]{1,0:T(8,128)(2,1)S(1)}, bf16[16,1792]{1,0:T(8,128)(2,1)S(1)}, u32[]{:S(2)}, u32[]{:S(2)}) collective-permute-start(bf16[16,1792]{1,0:T(8,128)(2,1)S(1)} %collective-permute-done.12), channel_id=1, source_target_pairs={{0,240},{16,0},{32,16},{48,32},{64,48},{80,64},{96,80},{112,96},{1... | collective-permute-start | bytes 172040 | tf_op jit(solution)/shard_map/ppermute | solution.py:22
  139.8 5.2 %collective-permute-start.7 = (bf16[16,1792]{1,0:T(8,128)(2,1)S(1)}, bf16[16,1792]{1,0:T(8,128)(2,1)S(1)}, u32[]{:S(2)}, u32[]{:S(2)}) collective-permute-start(bf16[16,1792]{1,0:T(8,128)(2,1)S(1)} %collective-permute-done.6), channel_id=1, source_target_pairs={{0,16},{16,32},{32,48},{48,64},{64,80},{80,96},{96,112},{112,128},... | collective-permute-start | bytes 172040 | tf_op jit(solution)/shard_map/ppermute | solution.py:20
  140.7 13.7 %collective-permute-start.14 = (bf16[16,1792]{1,0:T(8,128)(2,1)S(1)}, bf16[16,1792]{1,0:T(8,128)(2,1)S(1)}, u32[]{:S(2)}, u32[]{:S(2)}) collective-permute-start(bf16[16,1792]{1,0:T(8,128)(2,1)S(1)} %collective-permute-done.13), channel_id=1, source_target_pairs={{0,240},{16,0},{32,16},{48,32},{64,48},{80,64},{96,80},{112,96},{1... | collective-permute-start | bytes 172040 | tf_op jit(solution)/shard_map/ppermute | solution.py:22
Sparse Core Ops, SparseCore 0:
  88.8 53.4 all-gather.2
